TPU v7x, 512 devices: a whole 4x8x8 slice. The times are simulated.
512 devices in a mesh: dp: 8 (over y), ctx: 16 (over z_hi, x, core), head: 4 (over z_lo).
Axes of the slice: x: 4, y: 8, z: 8 (z_hi: 2, z_lo: 4; z = z_hi * 4 + z_lo), core: 2. Of those that a mesh axis runs over, the one named last changes fastest.
Arguments:
- queries: bfloat16 [65536, 3072], P(('dp', 'ctx'), 'head'), parts along dimension 0, may hold values from -6 to 6
- keys: bfloat16 [65536, 3072], P(('dp', 'ctx'), 'head'), parts along dimension 0, may hold values from -8 to 8
- values: bfloat16 [65536, 3072], P(('dp', 'ctx'), 'head'), parts along dimension 0, may hold values from -8 to 8
- pool_segments: int32 [128, 512], P(('dp', 'ctx')), parts along dimension 0, may hold values from 0 to 7, never falling along the last dimension, each value on 1 to 96 neighbouring positions
- window_map: int32 [128], P(('dp', 'ctx')), parts along dimension 0, may hold values from 0 to 15, each once
- ref_owner: int32 [8], P('dp'), parts along dimension 0, may hold values from 0 to 15
- ref_keys: bfloat16 [128, 512, 3072], P(('dp', 'ctx'), 'head'), parts along dimension 0, may hold values from -6 to 6
- ref_values: bfloat16 [128, 512, 3072], P(('dp', 'ctx'), 'head'), parts along dimension 0, may hold values from -6 to 6
- slopes: float32 [24], P('head'), may hold values from 0.02 to 2
Outputs:
- attended: bfloat16 [65536, 3072], P(('dp', 'ctx'), 'head'), parts along dimension 0
There are 8 independent parts, one for each index of `dp`. A program takes and returns all parts, laid end to end along the dimension named above; an argument that names none is the same for every part. Nothing has to cross between parts.
All inputs are finite; a program needn't handle non-finite values.
Results may differ from a plain program's by a relative error of at most 0.0021.
Values may be sent and summed in bfloat16 or wider, within the bound.
No kernel may reach another device: no remote copies, remote signals or barrier semaphores. Data moves between devices by JAX's collectives and lax.ppermute only.
A program may use at most 64 MiB of HBM per device.

v0:
```python
from functools import reduce
import math
import jax
import jax.numpy as jnp
from jax import lax
from jax.sharding import PartitionSpec as P

HD = 128
RATIO = 64


def spread(block, axis, source):
    block = jnp.where(lax.axis_index(axis) == source, block, jnp.zeros_like(block))
    return lax.psum(block, axis)


def group_terms(query_block, key_block, value_block, bias_term):
    score_scale = 1.0 / math.sqrt(HD)
    scores = (
        jnp.einsum("qhd,khd->hqk", query_block, key_block, preferred_element_type=jnp.float32)
        * score_scale
    )
    if bias_term is not None:
        scores = scores + bias_term[:, None, :]
    row_max = jnp.max(scores, axis=2)
    exp_terms = jnp.exp(scores - row_max[:, :, None])
    row_total = jnp.sum(exp_terms, axis=2)
    weights = exp_terms.astype(jnp.bfloat16)
    numerator = jnp.einsum("hqk,khd->qhd", weights, value_block, preferred_element_type=jnp.float32)
    return (row_max.T, row_total.T, numerator)


def combine_groups(group_list):
    ceiling = reduce(jnp.maximum, [triple[0] for triple in group_list])
    numerator = reduce(
        jnp.add, [jnp.exp(triple[0] - ceiling)[:, :, None] * triple[2] for triple in group_list]
    )
    denominator = reduce(
        jnp.add, [jnp.exp(triple[0] - ceiling) * triple[1] for triple in group_list]
    )
    return numerator / denominator[:, :, None]


def on_device(
    queries, keys, values, pool_segments, window_map, ref_owner, ref_keys, ref_values, slopes
):
    tok_rows = queries.shape[0]
    heads_here = queries.shape[1] // HD
    pool_count = tok_rows // RATIO
    member = (pool_segments[0][None, :] == jnp.arange(pool_count, dtype=jnp.int32)[:, None]).astype(
        jnp.bfloat16
    )
    counts = jnp.sum(member, axis=1, dtype=jnp.float32)
    pooled_keys = (
        jnp.dot(member, keys, preferred_element_type=jnp.float32) / counts[:, None]
    ).astype(jnp.bfloat16)
    pooled_values = (
        jnp.dot(member, values, preferred_element_type=jnp.float32) / counts[:, None]
    ).astype(jnp.bfloat16)
    window_tag = window_map.astype(jnp.bfloat16)
    all_keys, all_values, all_tags = (
        lax.all_gather(pooled_keys, "ctx", axis=0, tiled=True),
        lax.all_gather(pooled_values, "ctx", axis=0, tiled=True),
        lax.all_gather(window_tag, "ctx", axis=0, tiled=True),
    )
    ref_k, ref_v = (
        spread(ref_keys[0], "ctx", ref_owner[0]),
        spread(ref_values[0], "ctx", ref_owner[0]),
    )
    ref_k, ref_v = (
        lax.all_to_all(ref_k, "head", split_axis=1, concat_axis=0, tiled=True),
        lax.all_to_all(ref_v, "head", split_axis=1, concat_axis=0, tiled=True),
    )
    query_block = queries.reshape(tok_rows, heads_here, HD)
    key_block = keys.reshape(tok_rows, heads_here, HD)
    value_block = values.reshape(tok_rows, heads_here, HD)
    key_window = jnp.repeat(all_tags.astype(jnp.float32), pool_count)
    distance = jnp.abs(window_map[0].astype(jnp.float32) - key_window)
    bias_term = -slopes[:, None] * distance[None, :]
    group_list = [
        group_terms(query_block, key_block, value_block, None),
        group_terms(
            query_block,
            all_keys.reshape(-1, heads_here, HD),
            all_values.reshape(-1, heads_here, HD),
            bias_term,
        ),
        group_terms(
            query_block, ref_k.reshape(-1, heads_here, HD), ref_v.reshape(-1, heads_here, HD), None
        ),
    ]
    merged = combine_groups(group_list)
    return merged.reshape(tok_rows, heads_here * HD).astype(jnp.bfloat16)


def solution(mesh):
    return jax.shard_map(
        on_device,
        mesh=mesh,
        in_specs=(
            P(("dp", "ctx"), "head"),
            P(("dp", "ctx"), "head"),
            P(("dp", "ctx"), "head"),
            P(("dp", "ctx"), None),
            P(("dp", "ctx")),
            P("dp"),
            P(("dp", "ctx"), "head", None),
            P(("dp", "ctx"), "head", None),
            P("head"),
        ),
        out_specs=P(("dp", "ctx"), "head"),
        check_vma=False,
    )
```

profile of v0, /device:TPU:1, one launch (start us, length us, event | category | flops | bytes accessed | tf_op | source)
XLA Modules:
  0.0 324.7 jit_solution(16259391540248916373)
XLA Ops:
  7.4 1.2 copy.74
  8.5 1.1 copy.65
  10.4 1.3 dynamic-slice
  12.5 49.1 %all-reduce = bf16[16]{0:T(256)(128)(2,1)S(1)} all-reduce(bf16[16]{0:T(256)(128)(2,1)S(1)} %dynamic-update-slice), channel_id=1, replica_groups=mesh['dp'=8,'ctx'=16,'head'=4] {'ctx'}, use_global_device_ids=true, to_apply=%add | all-reduce | flops 16 | bytes 64
  61.8 1.3 copy.59
  63.1 141.0 %all-reduce.4.cloned.1.call-done = (bf16[128,4,768]{0,2,1:T(8,128)(2,1)}, bf16[128,4,768]{0,2,1:T(8,128)(2,1)}) async-done(((bf16[128,4,768]{0,2,1:T(8,128)(2,1)}, bf16[128,4,768]{0,2,1:T(8,128)(2,1)}), (bf16[128,4,768]{0,2,1:T(8,128)(2,1)}, bf16[128,4,768]{0,2,1:T(8,128)(2,1)})) %all-reduce.4.cloned.1.call-update) | async-done | bytes 1572880 | tf_op jit(solution)/shard_map/psum | solution.py:14
  204.2 4.2 %all-to-all-start.1 = ((bf16[128,4,768]{0,2,1:T(8,128)(2,1)}), bf16[128,4,768]{0,2,1:T(8,128)(2,1)}, u32[]{:S(2)}, u32[]{:S(2)}) async-start(bf16[128,4,768]{0,2,1:T(8,128)(2,1)} %get-tuple-element.5), calls=%async_computation.1 | async-start | bytes 1572864 | tf_op jit(solution)/shard_map/all_to_all | solution.py:72
  208.6 36.4 %all_gather.9 = bf16[128,768]{1,0:T(8,128)(2,1)S(1)} all-gather(bf16[8,768]{1,0:T(8,128)(2,1)S(1)} %fusion.20), channel_id=1, replica_groups=mesh['dp'=8,'ctx'=16,'head'=4] {'ctx'}, dimensions={0}, use_global_device_ids=true | all-gather | bytes 208896 | tf_op jit(solution)/shard_map/all_gather | solution.py:62
  245.5 1.0 bitcast_reduce_fusion.1
  246.5 4.9 %multiply_reduce_fusion = (f32[6,512]{1,0:T(8,128)S(1)}, f32[6,512,512]{1,2,0:T(8,128)}) fusion(bf16[512,6,128]{0,2,1:T(8,128)(2,1)S(1)} %bitcast.127, bf16[512,6,128]{0,2,1:T(8,128)(2,1)} %bitcast.132), kind=kOutput, calls=%fused_computation.4 | convolution fusion | flops 405795840 | bytes 7876608 | tf_op jit(solution)/shard_map/qhd,khd->hqk/dot_general | solution.py:20
  251.4 4.5 %all-to-all-start = ((bf16[128,4,768]{0,2,1:T(8,128)(2,1)}), bf16[128,4,768]{0,2,1:T(8,128)(2,1)}, u32[]{:S(2)}, u32[]{:S(2)}) async-start(bf16[128,4,768]{0,2,1:T(8,128)(2,1)} %get-tuple-element.6), calls=%async_computation | async-start | bytes 1572864 | tf_op jit(solution)/shard_map/all_to_all | solution.py:71
  256.1 1.4 copy.70
  257.5 35.2 %all_gather.11 = bf16[128,768]{1,0:T(8,128)(2,1)S(1)} all-gather(bf16[8,768]{1,0:T(8,128)(2,1)S(1)} %fusion.21), channel_id=1, replica_groups=mesh['dp'=8,'ctx'=16,'head'=4] {'ctx'}, dimensions={0}, use_global_device_ids=true | all-gather | bytes 208896 | tf_op jit(solution)/shard_map/all_gather | solution.py:63
  292.9 1.0 fusion.18
  293.9 4.0 %fusion.1 = f32[6,512]{1,0:T(8,128)S(1)} fusion(f32[6,512,512]{1,2,0:T(8,128)} %get-tuple-element.14, f32[6,512]{1,0:T(8,128)S(1)} %get-tuple-element.13), kind=kLoop, calls=%fused_computation.5 | loop fusion | flops 4715520 | bytes 6316032 | tf_op jit(solution)/shard_map/reduce_sum | solution.py:27
  298.5 2.5 fusion.7
  300.9 2.6 copy.75
  303.6 1.6 reshape.86
  305.2 2.6 copy.66
  307.9 2.4 reshape.83
  310.2 2.2 bitcast_reduce_fusion
  312.5 1.6 fusion.3
  314.1 1.9 fusion.5
  316.7 1.2 copy.76
  (36 shorter events, 3.5 us)
Async XLA Ops:
  6.5 197.6 %all-reduce.4.cloned.1.call-start = ((), (), s32[]{:S(2)}) async-start(), calls=%async_computation.2 | async-start | bytes 3145728 | tf_op jit(solution)/shard_map/psum | solution.py:14
  7.3 54.3 %copy-start.7 = (f32[6]{0:T(128)S(1)}, f32[6]{0:T(128)}, u32[]{:S(2)}) copy-start(f32[6]{0:T(128)} %param.17) | copy-start | bytes 76
  7.3 54.4 %copy-start.1 = (bf16[512,768]{1,0:T(8,128)(2,1)S(1)}, bf16[512,768]{1,0:T(8,128)(2,1)}, u32[]{:S(2)}) copy-start(bf16[512,768]{1,0:T(8,128)(2,1)} %param.10) | copy-start | bytes 2359300
  7.3 55.7 %copy-start.6 = (s32[1,512]{1,0:T(1,128)S(1)}, s32[1,512]{1,0:T(1,128)}, u32[]{:S(2)}) copy-start(s32[1,512]{1,0:T(1,128)} %param.12) | copy-start | bytes 6148
  9.7 235.5 %copy-start.4 = (bf16[512,768]{1,0:T(8,128)(2,1)S(1)}, bf16[512,768]{1,0:T(8,128)(2,1)}, u32[]{:S(2)}) copy-start(bf16[512,768]{1,0:T(8,128)(2,1)} %param.9) | copy-start | bytes 2359300
  204.2 47.2 %all-to-all-start.1 = ((bf16[128,4,768]{0,2,1:T(8,128)(2,1)}), bf16[128,4,768]{0,2,1:T(8,128)(2,1)}, u32[]{:S(2)}, u32[]{:S(2)}) async-start(bf16[128,4,768]{0,2,1:T(8,128)(2,1)} %get-tuple-element.5), calls=%async_computation.1 | async-start | bytes 1572864 | tf_op jit(solution)/shard_map/all_to_all | solution.py:72
  246.5 9.4 %copy-start.2 = (bf16[512,768]{1,0:T(8,128)(2,1)S(1)}, bf16[512,768]{1,0:T(8,128)(2,1)}, u32[]{:S(2)}) copy-start(bf16[512,768]{1,0:T(8,128)(2,1)} %param.11) | copy-start | bytes 2359300
  251.4 53.8 %all-to-all-start = ((bf16[128,4,768]{0,2,1:T(8,128)(2,1)}), bf16[128,4,768]{0,2,1:T(8,128)(2,1)}, u32[]{:S(2)}, u32[]{:S(2)}) async-start(bf16[128,4,768]{0,2,1:T(8,128)(2,1)} %get-tuple-element.6), calls=%async_computation | async-start | bytes 1572864 | tf_op jit(solution)/shard_map/all_to_all | solution.py:71
  293.9 4.6 %copy-start = (f32[6,512,512]{1,2,0:T(8,128)S(1)}, f32[6,512,512]{1,2,0:T(8,128)}, u32[]{:S(2)}) copy-start(f32[6,512,512]{1,2,0:T(8,128)} %get-tuple-element.14) | copy-start | bytes 18874372
  314.1 2.0 copy-start.5
  314.1 2.0 copy-start.3
Sparse Core Ops, SparseCore 0:
  10.3 193.8 all-reduce.3
where the time goes:
time: 325 us
  waiting for transfers between devices  141 us (43%)
  blocking collectives  121 us (37%)
  local copies, waits for them, and re-layouts  18.9 us (6%)
  between operations  15 us (5%)
  matrix products  13.6 us (4%)
  starting transfers between devices  8.65 us (3%)
  other arithmetic  6.88 us (2%)
    psum x1, waiting for transfers between devices, spread(): return lax.psum(block, axis)  141 us
    unnamed x1, blocking collectives  49.1 us
    all_gather x1, blocking collectives, on_device(): lax.all_gather(pooled_keys, 'ctx', axis=0, tiled=True)  36.4 us
    all_gather x1, blocking collectives, on_device(): lax.all_gather(pooled_values, 'ctx', axis=0, tiled=True)  35.2 us
    dot_general x3, matrix products, group_terms(): jnp.einsum('qhd,khd->hqk', query_block, key_block, preferred_element_type...  8.16 us
    reduce_sum x3, other arithmetic, group_terms(): row_total = jnp.sum(exp_terms, axis=2)  6.54 us
  transfers between devices with their start and end apart: 3, of which 1 were waited for; matrix products, arithmetic and copies ran while one was open for 7% of the time, Pallas kernels for 0%

commit v1 on v0

--- a/solution.py
+++ b/solution.py
@@ -60,7 +60,9 @@
     window_tag = window_map.astype(jnp.bfloat16)
     all_keys, all_values, all_tags = (
         lax.all_gather(pooled_keys, "ctx", axis=0, tiled=True),
-        lax.all_gather(pooled_values, "ctx", axis=0, tiled=True),
+        jnp.concatenate(
+            lax.all_to_all(jnp.stack([pooled_values] * lax.axis_size("ctx")), "ctx", 0, 0), axis=0
+        ),
         lax.all_gather(window_tag, "ctx", axis=0, tiled=True),
     )
     ref_k, ref_v = (

time: 325 us -> 293 us (0.902)
  blocking collectives: 121 us -> 79.3 us
  starting transfers between devices: 8.65 us -> 23.9 us
    all_gather x1 -> x0, blocking collectives: 35.2 us -> none  [on_device(): lax.all_gather(pooled_values, 'ctx', axis=0, tiled=True)]
    all_to_all x0 -> x1, starting transfers between devices: none -> 15.1 us  [on_device(): lax.all_to_all(jnp.stack([pooled_values] * lax.axis_size('ctx')), 'ctx',...]
    psum x1, waiting for transfers between devices: 141 us -> 132 us  [spread(): return lax.psum(block, axis)]
    unnamed x1, blocking collectives: 49.1 us -> 43.4 us
    all_to_all x1, waiting for transfers between devices: 0.01 us -> 5.54 us  [on_device(): lax.all_to_all(ref_k, 'head', split_axis=1, concat_axis=0, tiled=True)]
  transfers between devices with their start and end apart: 3 -> 4, of which waited for: 1 -> 2; matrix products, arithmetic and copies ran while one was open for 7% -> 8% of each run, Pallas kernels for 0% -> 0%
where the time goes in v1:
time: 293 us; the launch traced here: 292 us
  waiting for transfers between devices  138 us (47%)
  blocking collectives  79.3 us (27%)
  starting transfers between devices  23.9 us (8%)
  local copies, waits for them, and re-layouts  15.8 us (5%)
  between operations  14.9 us (5%)
  matrix products  12.9 us (4%)
  other arithmetic  7.64 us (3%)
    psum x1, waiting for transfers between devices, spread(): return lax.psum(block, axis)  132 us
    unnamed x1, blocking collectives  43.4 us
    all_gather x1, blocking collectives, on_device(): lax.all_gather(pooled_keys, 'ctx', axis=0, tiled=True)  35.9 us
    all_to_all x1, starting transfers between devices, on_device(): lax.all_to_all(jnp.stack([pooled_values] * lax.axis_size('ctx')), 'ctx',...  15.1 us
    dot_general x3, matrix products, group_terms(): jnp.einsum('qhd,khd->hqk', query_block, key_block, preferred_element_type...  7.47 us
    reduce_sum x3, other arithmetic, group_terms(): row_total = jnp.sum(exp_terms, axis=2)  7.29 us
    unnamed x24, local copies, waits for them, and re-layouts  6.07 us
  transfers between devices with their start and end apart: 4, of which 2 were waited for; matrix products, arithmetic and copies ran while one was open for 8% of the time, Pallas kernels for 0%

profile of v1, /device:TPU:1, one launch (start us, length us, event | category | flops | bytes accessed | tf_op | source)
XLA Modules:
  0.0 292.3 jit_solution(15864039277835257652)
XLA Ops:
  7.4 1.2 copy.74
  8.5 1.2 copy.65
  10.7 15.1 %all-to-all-start.1 = ((bf16[16,8,768]{2,1,0:T(8,128)(2,1)}), bf16[16,8,768]{2,1,0:T(8,128)(2,1)S(1)}, u32[]{:S(2)}, u32[]{:S(2)}) async-start(bf16[16,8,768]{2,1,0:T(8,128)(2,1)} %stack.2), calls=%async_computation.1 | async-start | bytes 393216 | tf_op jit(solution)/shard_map/all_to_all | solution.py:64
  26.4 1.3 dynamic-slice
  28.5 43.4 %all-reduce = bf16[16]{0:T(256)(128)(2,1)S(1)} all-reduce(bf16[16]{0:T(256)(128)(2,1)S(1)} %dynamic-update-slice), channel_id=1, replica_groups=mesh['dp'=8,'ctx'=16,'head'=4] {'ctx'}, use_global_device_ids=true, to_apply=%add | all-reduce | flops 16 | bytes 64
  71.9 132.4 %all-reduce.4.cloned.1.call-done = (bf16[128,4,768]{0,2,1:T(8,128)(2,1)}, bf16[128,4,768]{0,2,1:T(8,128)(2,1)}) async-done(((bf16[128,4,768]{0,2,1:T(8,128)(2,1)}, bf16[128,4,768]{0,2,1:T(8,128)(2,1)}), (bf16[128,4,768]{0,2,1:T(8,128)(2,1)}, bf16[128,4,768]{0,2,1:T(8,128)(2,1)})) %all-reduce.4.cloned.1.call-update) | async-done | bytes 1572880 | tf_op jit(solution)/shard_map/psum | solution.py:14
  204.3 4.2 %all-to-all-start.2 = ((bf16[128,4,768]{0,2,1:T(8,128)(2,1)}), bf16[128,4,768]{0,2,1:T(8,128)(2,1)}, u32[]{:S(2)}, u32[]{:S(2)}) async-start(bf16[128,4,768]{0,2,1:T(8,128)(2,1)} %get-tuple-element.5), calls=%async_computation.2 | async-start | bytes 1572864 | tf_op jit(solution)/shard_map/all_to_all | solution.py:74
  209.1 35.9 %all_gather.6 = bf16[128,768]{1,0:T(8,128)(2,1)S(1)} all-gather(bf16[8,768]{1,0:T(8,128)(2,1)S(1)} %fusion.20), channel_id=1, replica_groups=mesh['dp'=8,'ctx'=16,'head'=4] {'ctx'}, dimensions={0}, use_global_device_ids=true | all-gather | bytes 208896 | tf_op jit(solution)/shard_map/all_gather | solution.py:62
  245.2 1.4 copy.58
  246.7 3.7 %multiply_reduce_fusion = (f32[6,512]{1,0:T(8,128)S(1)}, f32[6,512,512]{1,2,0:T(8,128)}) fusion(bf16[512,6,128]{0,2,1:T(8,128)(2,1)S(1)} %bitcast.126, bf16[512,6,128]{0,2,1:T(8,128)(2,1)S(1)} %bitcast.132), kind=kOutput, calls=%fused_computation.4 | convolution fusion | flops 405795840 | bytes 7876608 | tf_op jit(solution)/shard_map/qhd,khd->hqk/dot_general | solution.py:20
  250.4 4.6 %all-to-all-start = ((bf16[128,4,768]{0,2,1:T(8,128)(2,1)}), bf16[128,4,768]{0,2,1:T(8,128)(2,1)}, u32[]{:S(2)}, u32[]{:S(2)}) async-start(bf16[128,4,768]{0,2,1:T(8,128)(2,1)} %get-tuple-element.6), calls=%async_computation | async-start | bytes 1572864 | tf_op jit(solution)/shard_map/all_to_all | solution.py:73
  255.0 1.6 bitcast_reduce_fusion.1
  256.6 2.3 copy.70
  258.9 1.8 fusion.18
  260.7 3.9 %fusion.1 = f32[6,512]{1,0:T(8,128)S(1)} fusion(f32[6,512,512]{1,2,0:T(8,128)} %get-tuple-element.14, f32[6,512]{1,0:T(8,128)S(1)} %get-tuple-element.13), kind=kLoop, calls=%fused_computation.5 | loop fusion | flops 4715520 | bytes 6316032 | tf_op jit(solution)/shard_map/reduce_sum | solution.py:27
  264.6 2.5 fusion.7
  267.3 1.7 copy.75
  269.4 5.5 %all-to-all-done = bf16[128,4,768]{0,2,1:T(8,128)(2,1)} async-done(((bf16[128,4,768]{0,2,1:T(8,128)(2,1)}), bf16[128,4,768]{0,2,1:T(8,128)(2,1)}, u32[]{:S(2)}, u32[]{:S(2)}) %all-to-all-start) | async-done | bytes 786464 | tf_op jit(solution)/shard_map/all_to_all | solution.py:73
  274.9 1.7 copy.66
  276.6 1.2 reshape.82
  277.8 2.2 bitcast_reduce_fusion
  280.1 1.6 fusion.3
  281.7 1.9 fusion.5
  284.3 1.2 copy.76
  (41 shorter events, 4.0 us)
Async XLA Ops:
  6.5 197.7 %all-reduce.4.cloned.1.call-start = ((), (), s32[]{:S(2)}) async-start(), calls=%async_computation.3 | async-start | bytes 3145728 | tf_op jit(solution)/shard_map/psum | solution.py:14
  7.3 2.4 copy-start.5
  7.3 2.5 copy-start.3
  7.3 64.5 %copy-start.6 = (f32[6]{0:T(128)S(1)}, f32[6]{0:T(128)}, u32[]{:S(2)}) copy-start(f32[6]{0:T(128)} %param.17) | copy-start | bytes 76
  8.5 200.1 %copy-start.2 = (bf16[512,768]{1,0:T(8,128)(2,1)S(1)}, bf16[512,768]{1,0:T(8,128)(2,1)}, u32[]{:S(2)}) copy-start(bf16[512,768]{1,0:T(8,128)(2,1)} %param.10) | copy-start | bytes 2359300
  10.7 61.1 %all-to-all-start.1 = ((bf16[16,8,768]{2,1,0:T(8,128)(2,1)}), bf16[16,8,768]{2,1,0:T(8,128)(2,1)S(1)}, u32[]{:S(2)}, u32[]{:S(2)}) async-start(bf16[16,8,768]{2,1,0:T(8,128)(2,1)} %stack.2), calls=%async_computation.1 | async-start | bytes 393216 | tf_op jit(solution)/shard_map/all_to_all | solution.py:64
  204.3 46.1 %all-to-all-start.2 = ((bf16[128,4,768]{0,2,1:T(8,128)(2,1)}), bf16[128,4,768]{0,2,1:T(8,128)(2,1)}, u32[]{:S(2)}, u32[]{:S(2)}) async-start(bf16[128,4,768]{0,2,1:T(8,128)(2,1)} %get-tuple-element.5), calls=%async_computation.2 | async-start | bytes 1572864 | tf_op jit(solution)/shard_map/all_to_all | solution.py:74
  250.4 14.2 %slice-start = ((s8[6291456]{0:T(1024)(128)(4,1)}), s8[2097152]{0:T(1024)(128)(4,1)S(1)}, s32[]{:S(2)}) async-start(s8[6291456]{0:T(1024)(128)(4,1)} %bitcast.124), calls=%async_computation.4 | async-start | bytes 4194304
  250.4 24.5 %all-to-all-start = ((bf16[128,4,768]{0,2,1:T(8,128)(2,1)}), bf16[128,4,768]{0,2,1:T(8,128)(2,1)}, u32[]{:S(2)}, u32[]{:S(2)}) async-start(bf16[128,4,768]{0,2,1:T(8,128)(2,1)} %get-tuple-element.6), calls=%async_computation | async-start | bytes 1572864 | tf_op jit(solution)/shard_map/all_to_all | solution.py:73
  258.9 5.7 %slice-start.1 = ((s8[6291456]{0:T(1024)(128)(4,1)}), s8[4194304]{0:T(1024)(128)(4,1)S(1)}, s32[]{:S(2)}) async-start(s8[6291456]{0:T(1024)(128)(4,1)} %bitcast.124), calls=%async_computation.5 | async-start | bytes 8388608
  260.7 3.9 %copy-start.1 = (bf16[512,768]{0,1:T(8,128)(2,1)S(1)}, bf16[512,768]{0,1:T(8,128)(2,1)}, u32[]{:S(2)}) copy-start(bf16[512,768]{0,1:T(8,128)(2,1)} %copy.70) | copy-start | bytes 2359300
  281.7 2.0 copy-start
  281.7 2.0 copy-start.4
Sparse Core Ops, SparseCore 0:
  10.3 193.8 all-reduce.3
